TPU v7x, 32 devices: a whole 2x2x4 slice. The times are simulated.
32 devices in a mesh: dyn: 4 (over x, core), col: 8 (over z, y).
Axes of the slice: x: 2, y: 2, z: 4, core: 2. Of those that a mesh axis runs over, the one named last changes fastest.
Arguments:
- planck_source: float32 [32, 32768], P(None, ('dyn', 'col')), may hold values from 0.5 to 1.5
- absorber_path: float32 [32, 32768], P(None, ('dyn', 'col')), may hold values from 0.2 to 3
- cloud_depth: float32 [32, 32768], P(None, ('dyn', 'col')), may hold values from 0 to 0.6
- span_map: int32 [32768], P(('dyn', 'col')), may hold values from 0 to 32767, as said below
- surface_source: float32 [32768], P(('dyn', 'col')), may hold values from 0.8 to 1.6
- interp_index: int32 [32, 32768], P(None, ('dyn', 'col')), may hold values from 0 to 830
- interp_weight: bfloat16 [4, 32, 32768], P(None, None, ('dyn', 'col')), may hold values from 0 to 0.5
- sunlit: int32 [32768], P(('dyn', 'col')), may hold values from 0 to 1, as said below
- sw_slot: int32 [32768], P(('dyn', 'col')), may hold values from 0 to 4095, as said below
- cos_zenith: float32 [32768], P(('dyn', 'col')), may hold values from 0.05 to 1
- albedo: float32 [32768], P(('dyn', 'col')), may hold values from 0.05 to 0.8
- table_lw: bfloat16 [256, 896], replicated, may hold values from 0.0029907227 to 3
- table_sw: bfloat16 [224, 896], replicated, may hold values from 0.0029 to 3
- planck_frac: float32 [256], replicated, may hold values from 0.0001 to 0.02
- solar_weight: float32 [224], replicated, may hold values from 0.0001 to 0.02
Outputs:
- heating_lw: float32 [32, 32768], P(None, ('dyn', 'col'))
- heating_sw: float32 [32, 32768], P(None, ('dyn', 'col'))
- sw_surface: float32 [16384], P(('dyn', 'col'))
Inputs may be any that keep to these rules, and one draw needn't show every extreme that they name: A permutation of the 32768 physics columns: column i goes to device span_map[i] // 1024 (flat index dyn * 8 + col), position span_map[i] % 1024. The number of columns that device s sends to device t depends only on (t - s) modulo the number of devices, is at most 64, and equals 64 for some pairs. In each dyn row the devices fall into pairs whose sunlit counts add up to 1024, so a dyn row holds 4096 sunlit columns; in every dyn row some device is sunlit in all its columns. For a sunlit column, sw_slot // 512 is the col index of the device of its dyn row that computes its shortwave and sw_slot % 512 its slot there. The sunlit columns of a dyn row, in order of device and column, are dealt to owners in turn from a drawn start; the values are distinct, every owner gets exactly 512, at most 128 from any one device and exactly that many from a fully sunlit one. For dark columns the value is arbitrary.
All inputs are finite; a program needn't handle non-finite values.
Results may differ from a plain program's by a relative error of at most 0.0003.
Values may be sent and summed in bfloat16 or wider, within the bound.
A program may use at most 128 MiB of HBM per device.

v0:
```python
from functools import partial

import jax
import jax.numpy as jnp
from jax import lax
from jax.sharding import PartitionSpec as P

TEMPS = 14
PRESS = 64


def corner_weights(index_row, weight_rows):
    entries = jnp.arange(TEMPS * PRESS, dtype=jnp.int32)[:, None]
    offsets = (0, 1, PRESS, PRESS + 1)
    mixing = jnp.zeros((TEMPS * PRESS, index_row.shape[0]), jnp.bfloat16)
    for corner in range(4):
        matches = entries == index_row[None, :] + offsets[corner]
        mixing = mixing + jnp.where(
            matches, weight_rows[corner][None, :], jnp.zeros((), jnp.bfloat16)
        )
    return mixing


def optical_depth(table, index_row, weight_rows, path_row, cloud_row):
    absorb = jnp.dot(
        table, corner_weights(index_row, weight_rows), preferred_element_type=jnp.float32
    )
    return path_row[None, :] * absorb + cloud_row[None, :]


def longwave(
    table, planck_frac, index_cols, weight_cols, path_cols, cloud_cols, planck_cols, surface_cols
):
    fraction = planck_frac[:, None]
    weight_levels = jnp.moveaxis(weight_cols, 0, 1)

    def longwave_downward(flux_in, inputs):
        index_row, weight_rows, path_row, cloud_row, planck_row = inputs
        optical = optical_depth(table, index_row, weight_rows, path_row, cloud_row)
        transmit = jnp.exp(-1.66 * optical)
        flux_out = flux_in * transmit + fraction * planck_row[None, :] * (1.0 - transmit)
        return (flux_out, (transmit, jnp.sum(flux_in - flux_out, axis=0)))

    initial = jnp.zeros((table.shape[0], index_cols.shape[1]), jnp.float32)
    bottom_down, (transmits, gained_down) = lax.scan(
        longwave_downward, initial, (index_cols, weight_levels, path_cols, cloud_cols, planck_cols)
    )

    def longwave_upward(flux_in, inputs):
        transmit, planck_row = inputs
        flux_out = flux_in * transmit + fraction * planck_row[None, :] * (1.0 - transmit)
        return (flux_out, jnp.sum(flux_in - flux_out, axis=0))

    ground = fraction * surface_cols[None, :]
    top_up, gained_up = lax.scan(longwave_upward, ground, (transmits, planck_cols), reverse=True)
    return gained_down + gained_up


def shortwave(
    table, solar_weight, index_cols, weight_cols, path_cols, cloud_cols, cosine_cols, albedo_cols
):
    weight_levels = jnp.moveaxis(weight_cols, 0, 1)

    def shortwave_downward(beam_in, inputs):
        index_row, weight_rows, path_row, cloud_row = inputs
        optical = optical_depth(table, index_row, weight_rows, path_row, cloud_row)
        beam_out = beam_in * jnp.exp(-optical / cosine_cols[None, :])
        return (beam_out, (jnp.exp(-1.66 * optical), jnp.sum(beam_in - beam_out, axis=0)))

    initial = solar_weight[:, None] * cosine_cols[None, :]
    ground_beam, (diffuse, gained_down) = lax.scan(
        shortwave_downward, initial, (index_cols, weight_levels, path_cols, cloud_cols)
    )

    def shortwave_upward(flux_in, transmit):
        flux_out = flux_in * transmit
        return (flux_out, jnp.sum(flux_in - flux_out, axis=0))

    top_up, gained_up = lax.scan(
        shortwave_upward, albedo_cols[None, :] * ground_beam, diffuse, reverse=True
    )
    ground_gain = jnp.sum(ground_beam, axis=0) * (1.0 - albedo_cols)
    return (gained_down + gained_up, ground_gain)


def by_blocks(function, arrays, block_cols):
    block_count = arrays[0].shape[-1] // block_cols

    def to_blocks(values):
        shaped = values.reshape(values.shape[:-1] + (block_count, block_cols))
        return jnp.moveaxis(shaped, -2, 0)

    def from_blocks(values):
        joined = jnp.moveaxis(values, 0, -2)
        return joined.reshape(joined.shape[:-2] + (block_count * block_cols,))

    results = lax.map(
        lambda block_args: function(*block_args), tuple((to_blocks(values) for values in arrays))
    )
    return jax.tree.map(from_blocks, results)


def deal_slots(holder, parties, capacity, columns):
    marked = (holder[:, None] == jnp.arange(parties, dtype=jnp.int32)[None, :]).astype(jnp.int32)
    placed = jnp.sum(jnp.cumsum(marked, axis=0) * marked, axis=1) - 1
    position = jnp.where(holder < parties, holder * capacity + placed, parties * capacity)
    filler = (
        jnp.full((parties * capacity,), columns, jnp.int32)
        .at[position]
        .set(jnp.arange(columns, dtype=jnp.int32), mode="drop")
    )
    return (position, filler)


def gather_cols(values, index, blank):
    return jnp.take(values, index, axis=-1, mode="fill", fill_value=blank)


def body(
    planck_source,
    absorber_path,
    cloud_depth,
    span_map,
    surface_source,
    interp_index,
    interp_weight,
    sunlit,
    sw_slot,
    cos_zenith,
    albedo,
    table_lw,
    table_sw,
    planck_frac,
    solar_weight,
):
    columns = span_map.shape[0]
    groups = lax.axis_size("dyn")
    devices = groups * lax.axis_size("col")
    capacity = 2 * columns // devices
    slots = devices * capacity
    position, filler = deal_slots(span_map // columns, devices, capacity, columns)
    planck_out = gather_cols(planck_source, filler, 0.0)
    path_out = gather_cols(absorber_path, filler, 0.0)
    cloud_out = gather_cols(cloud_depth, filler, 0.0)
    label_out = gather_cols(span_map % columns, filler, columns)[None, :].astype(jnp.float32)
    planck_in, path_in, cloud_in, label_in = (
        lax.all_to_all(planck_out, ("dyn", "col"), split_axis=1, concat_axis=1, tiled=True),
        lax.all_to_all(path_out, ("dyn", "col"), split_axis=1, concat_axis=1, tiled=True),
        lax.all_to_all(cloud_out, ("dyn", "col"), split_axis=1, concat_axis=1, tiled=True),
        lax.all_to_all(label_out, ("dyn", "col"), split_axis=1, concat_axis=1, tiled=True),
    )
    landing = label_in[0].astype(jnp.int32)
    anchor = (
        jnp.full((columns,), slots, jnp.int32)
        .at[landing]
        .set(jnp.arange(slots, dtype=jnp.int32), mode="drop")
    )
    planck_phys = jnp.take(planck_in, anchor, axis=1)
    path_phys = jnp.take(path_in, anchor, axis=1)
    cloud_phys = jnp.take(cloud_in, anchor, axis=1)
    block_cols = min(512, columns)
    lw_heat = by_blocks(
        partial(longwave, table_lw, planck_frac),
        (interp_index, interp_weight, path_phys, cloud_phys, planck_phys, surface_source),
        block_cols,
    )
    stripes = lax.axis_size("col")
    sw_count = columns // 2
    sw_capacity = columns // stripes
    holder = jnp.where(sunlit == 1, sw_slot // sw_count, stripes)
    sw_position, sw_filler = deal_slots(holder, stripes, sw_capacity, columns)
    sw_target = gather_cols(sw_slot % sw_count, sw_filler, sw_count)[None, :].astype(jnp.float32)
    levels = interp_index.shape[0]
    index_wide = interp_index.astype(jnp.float32)
    delivered = (
        lax.all_to_all(
            gather_cols(path_phys, sw_filler, 0.0), "col", split_axis=1, concat_axis=1, tiled=True
        ),
        lax.all_to_all(
            gather_cols(cloud_phys, sw_filler, 0.0), "col", split_axis=1, concat_axis=1, tiled=True
        ),
        lax.all_to_all(
            gather_cols(cos_zenith[None, :], sw_filler, 1.0),
            "col",
            split_axis=1,
            concat_axis=1,
            tiled=True,
        ),
        lax.all_to_all(
            gather_cols(albedo[None, :], sw_filler, 0.0),
            "col",
            split_axis=1,
            concat_axis=1,
            tiled=True,
        ),
        lax.all_to_all(
            gather_cols(index_wide, sw_filler, 0.0), "col", split_axis=1, concat_axis=1, tiled=True
        ),
        lax.all_to_all(sw_target, "col", split_axis=1, concat_axis=1, tiled=True),
    )
    weight_rows = interp_weight.reshape(4 * levels, columns)
    weight_in = lax.all_to_all(
        gather_cols(weight_rows, sw_filler, 0.0), "col", split_axis=1, concat_axis=1, tiled=True
    )
    arrival = delivered[5][0].astype(jnp.int32)
    compact = (
        jnp.full((sw_count,), columns, jnp.int32)
        .at[arrival]
        .set(jnp.arange(columns, dtype=jnp.int32), mode="drop")
    )
    path_sun, cloud_sun, cosine_sun, albedo_sun, index_sun = tuple(
        (jnp.take(values, compact, axis=1) for values in delivered[:5])
    )
    weight_sun = jnp.take(weight_in, compact, axis=1).reshape(4, levels, sw_count)
    index_sun = index_sun.astype(jnp.int32)
    sw_local, sw_surface = by_blocks(
        partial(shortwave, table_sw, solar_weight),
        (index_sun, weight_sun, path_sun, cloud_sun, cosine_sun[0], albedo_sun[0]),
        min(512, sw_count),
    )
    returned = lax.all_to_all(
        gather_cols(sw_local, arrival, 0.0), "col", split_axis=1, concat_axis=1, tiled=True
    )
    sw_heat = gather_cols(returned, sw_position, 0.0)
    lw_back = gather_cols(lw_heat, landing, 0.0)
    sw_back = gather_cols(sw_heat, landing, 0.0)
    lw_home, sw_home = (
        lax.all_to_all(lw_back, ("dyn", "col"), split_axis=1, concat_axis=1, tiled=True),
        lax.all_to_all(sw_back, ("dyn", "col"), split_axis=1, concat_axis=1, tiled=True),
    )
    heating_lw = jnp.take(lw_home, position, axis=1)
    heating_sw = jnp.take(sw_home, position, axis=1)
    return (heating_lw, heating_sw, sw_surface)


def solution(mesh):
    in_specs = (
        P(None, ("dyn", "col")),
        P(None, ("dyn", "col")),
        P(None, ("dyn", "col")),
        P(("dyn", "col")),
        P(("dyn", "col")),
        P(None, ("dyn", "col")),
        P(None, None, ("dyn", "col")),
        P(("dyn", "col")),
        P(("dyn", "col")),
        P(("dyn", "col")),
        P(("dyn", "col")),
        P(),
        P(),
        P(),
        P(),
    )
    out_specs = (P(None, ("dyn", "col")), P(None, ("dyn", "col")), P(("dyn", "col")))
    return jax.shard_map(body, mesh=mesh, in_specs=in_specs, out_specs=out_specs, check_vma=False)
```

profile of v0, /device:TPU:0, one launch (start us, length us, event | category | flops | bytes accessed | tf_op | source)
XLA Modules:
  0.0 711.4 jit_solution(1616509870945806447)
XLA Ops:
  1.4 2.3 reduce-window.16
  4.8 4.3 scatter_custom_fusion.2
  9.1 4.5 gather_fusion.5
  14.3 4.5 gather_fusion.2
  19.4 7.3 %all-to-all-start.6 = ((f32[1,8,128]{2,0,1:T(1,128)}), f32[1,8,128]{2,0,1:T(1,128)S(1)}, u32[]{:S(2)}, u32[]{:S(2)}) async-start(f32[1,8,128]{2,0,1:T(1,128)} %bitcast.61), calls=%async_computation.6 | async-start | bytes 8192 | tf_op jit(solution)/shard_map/all_to_all | solution.py:182
  26.7 4.5 gather_fusion.1
  31.3 9.0 %reduce-window.14 = s32[32,8,128]{2,1,0:T(8,128)S(1)} reduce-window(s32[32,8,128]{2,1,0:T(8,128)S(1)} %fusion.56, s32[]{:T(128)} %constant.419.clone.1), window={size=1x1x128 pad=0_0x0_0x127_0}, to_apply=%region_0.1 | reduce-window | flops 4161536 | bytes 262148 | tf_op jit(solution)/shard_map/reduce-window
  41.4 4.3 scatter_custom_fusion
  45.7 8.6 %gather_fusion = s32[2048]{0:T(1024)S(1)} fusion(s32[1024]{0:T(1024)S(1)} %get-tuple-element.830, s32[2048]{0:T(1024)S(1)} %fusion.60), kind=kCustom, calls=%fused_computation.19 | custom fusion | bytes 24576 | tf_op jit(solution)/shard_map/jit(_take)/gather | solution.py:116
  55.7 7.6 %gather_fusion.11 = f32[2048,32]{1,0:T(8,128)} fusion(f32[32,1024]{0,1:T(8,128)S(1)} %copy.107, s32[2048]{0:T(1024)S(1)} %fusion.60), kind=kCustom, calls=%fused_computation.6.clone | custom fusion | bytes 532480 | tf_op jit(solution)/shard_map/jit(_take)/gather | solution.py:116
  63.5 7.6 %gather_fusion.7 = f32[2048,32]{1,0:T(8,128)} fusion(f32[32,1024]{0,1:T(8,128)S(1)} %copy.99, s32[2048]{0:T(1024)S(1)} %fusion.60), kind=kCustom, calls=%fused_computation.clone | custom fusion | bytes 532480 | tf_op jit(solution)/shard_map/jit(_take)/gather | solution.py:116
  71.3 7.6 %gather_fusion.9 = f32[2048,32]{1,0:T(8,128)} fusion(f32[32,1024]{0,1:T(8,128)S(1)} %copy.103, s32[2048]{0:T(1024)S(1)} %fusion.60), kind=kCustom, calls=%fused_computation.5.clone | custom fusion | bytes 532480 | tf_op jit(solution)/shard_map/jit(_take)/gather | solution.py:116
  78.9 6.0 all-to-all-start.5
  88.1 4.3 gather_fusion.3
  92.4 6.0 all-to-all-start.11
  101.6 3.2 all-to-all-done.11
  104.8 3.3 all-to-all-start.1
  118.4 4.0 gather_fusion.18
  122.6 5.8 all-to-all-start.3
  128.4 4.3 scatter_custom_fusion.3
  132.8 2.3 gather_fusion.15
  135.1 4.0 all-to-all-done.3
  139.1 2.6 all-to-all-start.2
  141.7 2.3 gather_fusion.22
  145.5 6.8 all-to-all-done.2
  152.3 3.3 all-to-all-start
  155.6 8.2 %scatter_custom_fusion.1 = s32[1024]{0:T(1024)S(1)} fusion(s32[2048]{0:T(1024)S(1)} %bitcast.349, s32[2048]{0:T(1024)S(1)} %iota.37, s32[]{:T(128)} %constant.428.clone.1), kind=kCustom, calls=%fused_computation.217 | custom fusion | bytes 4100 | tf_op jit(solution)/shard_map/scatter | solution.py:156
  168.1 2.8 gather_fusion.12
  170.9 4.0 gather_fusion.10
  174.9 5.8 all-to-all-start.9
  180.7 2.2 reduce.26
  183.4 4.0 gather_fusion.8
  188.9 4.0 gather_fusion.20
  192.9 4.0 gather_fusion.16
  196.8 2.6 broadcast_select_fusion.5
  201.3 6.0 all-to-all-start.10
  210.6 4.0 all-to-all-done.10
  214.6 3.4 all-to-all-start.7
  222.3 2.9 all-to-all-done.7
  225.3 3.4 all-to-all-start.8
  232.5 3.5 all-to-all-done.8
  237.7 128.5 %while.122 = (s32[]{:T(128)}, f32[224,512]{1,0:T(8,128)S(1)}, f32[32,224,512]{2,1,0:T(8,128)}, f32[32,512]{1,0:T(8,128)S(1)}, f32[32,512]{1,0:T(8,128)S(1)}, /*i...) while((s32[]{:T(128)}, f32[224,512]{1,0:T(8,128)S(1)}, ...), condition=%wide.region_20.26_spmd, body=%wide.region_18.25_spmd.sunk | while | flops 213779456 | bytes 2748633 | solution.py:71
  242.6 2.2 subtract_reduce_fusion.8
  274.8 2.2 subtract_reduce_fusion.8
  290.8 2.2 subtract_reduce_fusion.8
  327.0 2.2 subtract_reduce_fusion.8
  335.0 2.2 subtract_reduce_fusion.8
  366.9 43.4 %while.123 = (s32[]{:T(128)}, f32[224,512]{1,0:T(8,128)S(1)}, f32[32,512]{1,0:T(8,128)S(1)}, f32[32,224,512]{2,1,0:T(8,128)}, s32[]{:T(128)}, /*index=5*/s32[]{:T(128)}, s32[]{:T(128)}) while((s32[]{:T(128)}, f32[224,512]{1,0:T(8,128)S(1)}, f32[32,512]{1,0:T(8,128)S(1)}, f32[32,224,512]{2,1,0:T(8,128)}, s32[]{:T(128)}, ...), condition=%wide.region_23.29_spmd, body=%wide.region_21.28_spmd.sunk | while | flops 343555 | bytes 1382505 | solution.py:79
  410.4 2.8 gather_fusion.6
  414.1 3.6 all-to-all-start.12
  417.7 235.2 %while.121 = (s32[]{:T(128)}, f32[2,32,512]{2,1,0:T(8,128)S(1)}, s32[2,32,512]{2,0,1:T(2,128)S(1)}, bf16[2,4,32,512]{3,1,2,0:T(4,128)(2,1)S(1)}, f32[2,32,512]{2...) while((s32[]{:T(128)}, f32[2,32,512]{2,1,0:T(8,128)S(1)}, ...), condition=%wide.region_12.15_spmd, body=%wide.region_5.14_spmd.sunk | while | flops 244728320 | bytes 6502201 | solution.py:97
  418.0 73.0 %while.124 = (s32[]{:T(128)}, f32[256,512]{1,0:T(8,128)S(1)}, f32[32,256,512]{2,1,0:T(8,128)}, f32[32,512]{1,0:T(8,128)S(1)}, f32[32,512]{1,0:T(8,128)S(1)}, /*i...) while((s32[]{:T(128)}, f32[256,512]{1,0:T(8,128)S(1)}, ...), condition=%wide.region_8.10_spmd.clone, body=%wide.region_6.9_spmd.clone.sunk | while | flops 243663872 | bytes 3138799 | solution.py:45
  491.1 44.2 %while.125 = (s32[]{:T(128)}, f32[256,512]{1,0:T(8,128)S(1)}, f32[32,512]{1,0:T(8,128)S(1)}, f32[32,256,512]{2,1,0:T(8,128)}, f32[256,1]{0,1:T(1,128)S(1)}, /*in...) while((s32[]{:T(128)}, f32[256,512]{1,0:T(8,128)S(1)}, f32[32,512]{1,0:T(8,128)S(1)}, ...), condition=%wide.region_11.13_spmd, body=%wide.region_9.12_spmd.sunk | while | flops 916995 | bytes 1586301 | solution.py:55
  535.6 73.0 %while.124 = (s32[]{:T(128)}, f32[256,512]{1,0:T(8,128)S(1)}, f32[32,256,512]{2,1,0:T(8,128)}, f32[32,512]{1,0:T(8,128)S(1)}, f32[32,512]{1,0:T(8,128)S(1)}, /*i...) while((s32[]{:T(128)}, f32[256,512]{1,0:T(8,128)S(1)}, ...), condition=%wide.region_8.10_spmd.clone, body=%wide.region_6.9_spmd.clone.sunk | while | flops 243663872 | bytes 3138799 | solution.py:45
  608.7 44.2 %while.125 = (s32[]{:T(128)}, f32[256,512]{1,0:T(8,128)S(1)}, f32[32,512]{1,0:T(8,128)S(1)}, f32[32,256,512]{2,1,0:T(8,128)}, f32[256,1]{0,1:T(1,128)S(1)}, /*in...) while((s32[]{:T(128)}, f32[256,512]{1,0:T(8,128)S(1)}, f32[32,512]{1,0:T(8,128)S(1)}, ...), condition=%wide.region_11.13_spmd, body=%wide.region_9.12_spmd.sunk | while | flops 916995 | bytes 1586301 | solution.py:55
  653.1 5.5 gather_fusion.13
  658.8 2.8 gather_fusion.23
  661.9 7.6 %gather_fusion.24 = f32[2048,32]{1,0:T(8,128)} fusion(f32[32,1024]{0,1:T(8,128)S(1)} %select_bitcast_fusion.1, s32[2048]{0:T(1024)S(1)} %fusion.61), kind=kCustom, calls=%fused_computation.8.clone | custom fusion | bytes 532480 | tf_op jit(solution)/shard_map/jit(_take)/gather | solution.py:116
  672.5 5.7 all-to-all-start.13
  679.5 9.3 %all-to-all-done.13 = f32[32,1,2048]{2,1,0:T(1,128)S(1)} async-done(((f32[32,1,2048]{2,1,0:T(1,128)}), f32[32,1,2048]{2,1,0:T(1,128)S(1)}, u32[]{:S(2)}, u32[]{:S(2)}) %all-to-all-start.13) | async-done | bytes 262176 | tf_op jit(solution)/shard_map/all_to_all | solution.py:229
  688.8 2.6 all-to-all-start.4
  693.3 8.8 %all-to-all-done.4 = f32[32,1,2048]{2,1,0:T(1,128)S(1)} async-done(((f32[32,1,2048]{2,1,0:T(1,128)}), f32[32,1,2048]{2,1,0:T(1,128)S(1)}, u32[]{:S(2)}, u32[]{:S(2)}) %all-to-all-start.4) | async-done | bytes 262176 | tf_op jit(solution)/shard_map/all_to_all | solution.py:228
  703.9 2.8 gather_fusion.25
  706.7 2.8 gather_fusion.14
  (1190 shorter events, 445.4 us)
Async XLA Ops:
  0.6 8.5 %copy-start = (f32[1024]{0:T(1024)S(1)}, f32[1024]{0:T(1024)}, u32[]{:S(2)}) copy-start(f32[1024]{0:T(1024)} %param.45) | copy-start | bytes 12292
  4.8 8.9 %copy-start.16 = (s32[1024]{0:T(1024)}, s32[1024]{0:T(1024)S(1)}, u32[]{:S(2)}) copy-start(s32[1024]{0:T(1024)S(1)} %get-tuple-element.807) | copy-start | bytes 12292
  9.1 5.2 copy-start.2
  14.3 40.7 %copy-start.10 = (pred[1024]{0:T(1024)(128)(4,1)}, pred[1024]{0:T(1024)(128)(4,1)S(1)}, u32[]{:S(2)}) copy-start(pred[1024]{0:T(1024)(128)(4,1)S(1)} %get-tuple-element.809) | copy-start | bytes 3076
  19.4 59.5 %all-to-all-start.6 = ((f32[1,8,128]{2,0,1:T(1,128)}), f32[1,8,128]{2,0,1:T(1,128)S(1)}, u32[]{:S(2)}, u32[]{:S(2)}) async-start(f32[1,8,128]{2,0,1:T(1,128)} %bitcast.61), calls=%async_computation.6 | async-start | bytes 8192 | tf_op jit(solution)/shard_map/all_to_all | solution.py:182
  26.7 4.5 copy-start.21
  41.4 4.3 copy-start.14
  45.7 9.8 %copy-start.6 = (f32[32,1024]{1,0:T(8,128)S(1)}, f32[32,1024]{1,0:T(8,128)}, u32[]{:S(2)}) copy-start(f32[32,1024]{1,0:T(8,128)} %param.35) | copy-start | bytes 393220
  54.3 9.0 %copy-start.7 = (f32[32,1024]{1,0:T(8,128)S(1)}, f32[32,1024]{1,0:T(8,128)}, u32[]{:S(2)}) copy-start(f32[32,1024]{1,0:T(8,128)} %param.36) | copy-start | bytes 393220
  63.3 7.8 %copy-start.8 = (f32[32,1024]{1,0:T(8,128)S(1)}, f32[32,1024]{1,0:T(8,128)}, u32[]{:S(2)}) copy-start(f32[32,1024]{1,0:T(8,128)} %param.37) | copy-start | bytes 393220
  78.9 13.5 %all-to-all-start.5 = ((f32[1,8,128]{2,0,1:T(1,128)}), f32[1,8,128]{2,0,1:T(1,128)S(1)}, u32[]{:S(2)}, u32[]{:S(2)}) async-start(f32[1,8,128]{2,0,1:T(1,128)} %bitcast.57), calls=%async_computation.5 | async-start | bytes 8192 | tf_op jit(solution)/shard_map/all_to_all | solution.py:199
  86.9 22.4 %copy-start.5 = (s32[32,1024]{1,0:T(8,128)S(1)}, s32[32,1024]{1,0:T(8,128)}, u32[]{:S(2)}) copy-start(s32[32,1024]{1,0:T(8,128)} %param.40) | copy-start | bytes 393220
  92.4 12.5 %all-to-all-start.11 = ((f32[1,8,128]{2,0,1:T(1,128)}), f32[1,8,128]{2,0,1:T(1,128)S(1)}, u32[]{:S(2)}, u32[]{:S(2)}) async-start(f32[1,8,128]{2,0,1:T(1,128)} %bitcast.346), calls=%async_computation.11 | async-start | bytes 8192 | tf_op jit(solution)/shard_map/all_to_all | solution.py:189
  104.8 17.8 %all-to-all-start.1 = ((f32[1,32,64]{2,0,1:T(1,128)}), f32[1,32,64]{2,0,1:T(1,128)}, u32[]{:S(2)}, u32[]{:S(2)}) async-start(f32[1,32,64]{2,0,1:T(1,128)} %convert_element_type.80), calls=%async_computation.1 | async-start | bytes 32768 | tf_op jit(solution)/shard_map/all_to_all | solution.py:150
  116.8 5.6 copy-start.3
  117.2 5.5 copy-start.22
  122.6 16.4 %all-to-all-start.3 = ((f32[32,1,2048]{2,1,0:T(1,128)}), f32[32,1,2048]{2,1,0:T(1,128)S(1)}, u32[]{:S(2)}, u32[]{:S(2)}) async-start(f32[32,1,2048]{2,1,0:T(1,128)} %reshape.702), calls=%async_computation.3 | async-start | bytes 524288 | tf_op jit(solution)/shard_map/all_to_all | solution.py:147
  135.1 9.5 %copy-start.23 = (f32[224]{0:T(256)S(1)}, f32[224]{0:T(256)}, u32[]{:S(2)}) copy-start(f32[224]{0:T(256)} %param.49) | copy-start | bytes 2692
  139.1 13.2 %all-to-all-start.2 = ((f32[32,1,2048]{2,1,0:T(1,128)}), f32[32,1,2048]{2,1,0:T(1,128)S(1)}, u32[]{:S(2)}, u32[]{:S(2)}) async-start(f32[32,1,2048]{2,1,0:T(1,128)} %reshape.700), calls=%async_computation.2 | async-start | bytes 524288 | tf_op jit(solution)/shard_map/all_to_all | solution.py:149
  152.3 22.6 %all-to-all-start = ((f32[32,1,2048]{2,1,0:T(1,128)}), f32[32,1,2048]{2,1,0:T(1,128)}, u32[]{:S(2)}, u32[]{:S(2)}) async-start(f32[32,1,2048]{2,1,0:T(1,128)} %reshape.698), calls=%async_computation | async-start | bytes 524288 | tf_op jit(solution)/shard_map/all_to_all | solution.py:148
  174.9 26.4 %all-to-all-start.9 = ((bf16[128,8,128]{0,2,1:T(8,128)(2,1)}), bf16[128,8,128]{0,2,1:T(8,128)(2,1)S(1)}, u32[]{:S(2)}, u32[]{:S(2)}) async-start(bf16[128,8,128]{0,2,1:T(8,128)(2,1)} %broadcast_select_fusion.11), calls=%async_computation.9 | async-start | bytes 524288 | tf_op jit(solution)/shard_map/all_to_all | solution.py:202
  188.9 8.0 %copy-start.11 = (pred[1024]{0:T(1024)(128)(4,1)S(1)}, pred[1024]{0:T(1024)(128)(4,1)}, u32[]{:S(2)}) copy-start(pred[1024]{0:T(1024)(128)(4,1)} %copy-done.10) | copy-start | bytes 3076
  201.3 13.3 %all-to-all-start.10 = ((f32[32,8,128]{2,0,1:T(8,128)}), f32[32,8,128]{2,0,1:T(8,128)S(1)}, u32[]{:S(2)}, u32[]{:S(2)}) async-start(f32[32,8,128]{2,0,1:T(8,128)} %copy.123), calls=%async_computation.10 | async-start | bytes 262144 | tf_op jit(solution)/shard_map/all_to_all | solution.py:179
  214.6 10.7 %all-to-all-start.7 = ((f32[32,8,128]{2,0,1:T(8,128)}), f32[32,8,128]{2,0,1:T(8,128)S(1)}, u32[]{:S(2)}, u32[]{:S(2)}) async-start(f32[32,8,128]{2,0,1:T(8,128)} %copy.116), calls=%async_computation.7 | async-start | bytes 262144 | tf_op jit(solution)/shard_map/all_to_all | solution.py:176
  225.3 10.7 %all-to-all-start.8 = ((f32[32,8,128]{2,0,1:T(8,128)}), f32[32,8,128]{2,0,1:T(8,128)S(1)}, u32[]{:S(2)}, u32[]{:S(2)}) async-start(f32[32,8,128]{2,0,1:T(8,128)} %copy.119), calls=%async_computation.8 | async-start | bytes 262144 | tf_op jit(solution)/shard_map/all_to_all | solution.py:196
  366.9 43.6 %copy-start.13 = (s32[1024]{0:T(1024)S(1)}, s32[1024]{0:T(1024)}, u32[]{:S(2)}) copy-start(s32[1024]{0:T(1024)} %broadcast_clamp_fusion) | copy-start | bytes 12292
  410.2 3.2 copy-start.18
  410.2 7.5 %copy-start.4 = (f32[256]{0:T(256)S(1)}, f32[256]{0:T(256)}, u32[]{:S(2)}) copy-start(f32[256]{0:T(256)} %param.48) | copy-start | bytes 3076
  410.3 7.5 %copy-start.9 = (f32[2,32,512]{2,1,0:T(8,128)S(1)}, f32[2,32,512]{2,1,0:T(8,128)}, u32[]{:S(2)}) copy-start(f32[2,32,512]{2,1,0:T(8,128)} %custom-call.54) | copy-start | bytes 393220
  410.3 7.5 %copy-start.24 = (bf16[256,896]{1,0:T(8,128)(2,1)S(1)}, bf16[256,896]{1,0:T(8,128)(2,1)}, u32[]{:S(2)}) copy-start(bf16[256,896]{1,0:T(8,128)(2,1)} %param.46) | copy-start | bytes 1376260
  414.1 244.5 %all-to-all-start.12 = ((f32[32,8,128]{2,0,1:T(8,128)}), f32[32,8,128]{2,0,1:T(8,128)S(1)}, u32[]{:S(2)}, u32[]{:S(2)}) async-start(f32[32,8,128]{2,0,1:T(8,128)} %broadcast_select_fusion.12), calls=%async_computation.12 | async-start | bytes 262144 | tf_op jit(solution)/shard_map/all_to_all | solution.py:221
  652.9 5.9 copy-start.12
  653.1 8.5 %copy-start.20 = (pred[1024]{0:T(1024)(128)(4,1)S(1)}, pred[1024]{0:T(1024)(128)(4,1)}, u32[]{:S(2)}) copy-start(pred[1024]{0:T(1024)(128)(4,1)} %get-tuple-element.806) | copy-start | bytes 3076
  661.6 7.8 %copy-start.17 = (pred[2048]{0:T(1024)(128)(4,1)S(1)}, pred[2048]{0:T(1024)(128)(4,1)}, u32[]{:S(2)}) copy-start(pred[2048]{0:T(1024)(128)(4,1)} %compare_and_fusion) | copy-start | bytes 6148
  672.5 18.9 %copy-start.15 = (s32[1024]{0:T(1024)S(1)}, s32[1024]{0:T(1024)}, u32[]{:S(2)}) copy-start(s32[1024]{0:T(1024)} %copy-done.14) | copy-start | bytes 12292
  672.5 16.3 %all-to-all-start.13 = ((f32[32,1,2048]{2,1,0:T(1,128)}), f32[32,1,2048]{2,1,0:T(1,128)S(1)}, u32[]{:S(2)}, u32[]{:S(2)}) async-start(f32[32,1,2048]{2,1,0:T(1,128)} %reshape.706), calls=%async_computation.13 | async-start | bytes 524288 | tf_op jit(solution)/shard_map/all_to_all | solution.py:229
  688.8 13.2 %all-to-all-start.4 = ((f32[32,1,2048]{2,1,0:T(1,128)}), f32[32,1,2048]{2,1,0:T(1,128)S(1)}, u32[]{:S(2)}, u32[]{:S(2)}) async-start(f32[32,1,2048]{2,1,0:T(1,128)} %reshape.704), calls=%async_computation.4 | async-start | bytes 524288 | tf_op jit(solution)/shard_map/all_to_all | solution.py:228
  703.5 6.0 copy-start.19
  706.7 4.7 copy-start.1
where the time goes:
time: 720 us; the launch traced here: 711 us
  local copies, waits for them, and re-layouts  254 us (35%)
  other arithmetic  191 us (27%)
  matrix products  149 us (21%)
  starting transfers between devices  64.5 us (9%)
  waiting for transfers between devices  42.5 us (6%)
  loops' own time  8.49 us (1%)
    dot_general x96, matrix products, optical_depth(): jnp.dot(table, corner_weights(index_row, weight_rows), preferred_element_...  149 us
    reduce_sum x64, other arithmetic, longwave_upward(): return (flux_out, jnp.sum(flux_in - flux_out, axis=0))  81.8 us
    gather x16, local copies, waits for them, and re-layouts, gather_cols(): return jnp.take(values, index, axis=-1, mode='fill', fill_value=blank)  80 us
    dynamic_update_slice x256, local copies, waits for them, and re-layouts, longwave(): lax.scan(longwave_downward, initial, (index_cols, weight_levels, path_col...  63 us
    reduce_sum x32, other arithmetic, shortwave_upward(): return (flux_out, jnp.sum(flux_in - flux_out, axis=0))  40.9 us
    slice x96, local copies, waits for them, and re-layouts, corner_weights(): weight_rows[corner][None, :]  31.1 us
    dynamic_update_slice x32, other arithmetic, shortwave(): lax.scan(shortwave_downward, initial, (index_cols, weight_levels, path_co...  27.3 us
  transfers between devices with their start and end apart: 14, of which 8 were waited for; matrix products, arithmetic and copies ran while one was open for 53% of the time, Pallas kernels for 0%

commit v1 on v0

v1 whole, which is shorter than its diff:
```python
import functools
import math

import jax
import jax.numpy as jnp
from jax import lax
from jax.experimental import pallas as pl
from jax.experimental.pallas import tpu as pltpu
from jax.sharding import PartitionSpec as P

TEMPS = 14
PRESS = 64
LANES = 128
WIDE = 256
AXES = ("dyn", "col")
LOG2E = math.log2(math.e)
DIFFUSE = -1.66 * LOG2E
VMEM = pl.BlockSpec(memory_space=pltpu.VMEM)


def iota(shape, dim):
    return lax.broadcasted_iota(jnp.int32, shape, dim)


def hot(mask):
    return jnp.where(mask, 1.0, 0.0).astype(jnp.bfloat16)


def contract(a, b, dims):
    return lax.dot_general(a, b, (dims, ((), ())), preferred_element_type=jnp.float32)


def pieces(values):
    high = values.astype(jnp.bfloat16)
    rest = values - high.astype(jnp.float32)
    middle = rest.astype(jnp.bfloat16)
    low = (rest - middle.astype(jnp.float32)).astype(jnp.bfloat16)
    return high, middle, low


def plan_kernel(devices, capacity, span_ref, label_ref, place_ref):
    columns = span_ref.shape[1]
    span = span_ref[...]
    target = span >> (columns.bit_length() - 1)
    where = span & (columns - 1)
    marked = target == iota((devices, columns), 0)
    before = hot(iota((columns, columns), 0) < iota((columns, columns), 1))
    counts = contract(hot(marked), before, ((1,), (0,)))
    rank = jnp.sum(jnp.where(marked, counts, 0.0), axis=0, keepdims=True).astype(jnp.int32)
    place_ref[...] = target * capacity + rank
    ranked = hot(rank == iota((LANES, columns), 0))
    high = jnp.where(marked, ((where >> 5) + 1).astype(jnp.float32), 0.0).astype(jnp.bfloat16)
    low = jnp.where(marked, (where & 31).astype(jnp.float32), 0.0).astype(jnp.bfloat16)
    dims = ((1,), (1,))
    label_ref[...] = contract(high, ranked, dims) * 32.0 + contract(low, ranked, dims) - 32.0


def pack_kernel(
    devices, capacity, label_ref, index_ref, weight_ref, surface_ref, cosine_ref, albedo_ref,
    sunlit_ref, slot_ref, out_ref, rows, chosen,
):
    columns = index_ref.shape[1]
    levels = index_ref.shape[0]
    base = 6 * levels
    index = index_ref[...]
    rows[0 : 4 * levels, :] = weight_ref[...]
    rows[4 * levels : 5 * levels, :] = (index >> 6).astype(jnp.float32).astype(jnp.bfloat16)
    rows[5 * levels : 6 * levels, :] = (index & (PRESS - 1)).astype(jnp.float32).astype(jnp.bfloat16)
    slot = slot_ref[...]
    scalars = [
        *pieces(surface_ref[...]),
        *pieces(cosine_ref[...]),
        *pieces(albedo_ref[...]),
        sunlit_ref[...].astype(jnp.float32).astype(jnp.bfloat16),
        (slot >> 7).astype(jnp.float32).astype(jnp.bfloat16),
        (slot & (LANES - 1)).astype(jnp.float32).astype(jnp.bfloat16),
    ]
    scalars = [values.astype(jnp.float32) for values in scalars]
    blank = jnp.zeros((16 - len(scalars), columns), jnp.float32)
    rows[base : base + 16, :] = jnp.concatenate(scalars + [blank], axis=0).astype(jnp.bfloat16)
    rows[base + 16 :, :] = jnp.zeros((WIDE - base - 16, columns), jnp.bfloat16)
    labels = label_ref[...]
    if devices < LANES:
        labels = jnp.concatenate(
            [labels, jnp.zeros((LANES - devices, LANES), jnp.float32)], axis=0
        )
    asked = jnp.transpose(labels).astype(jnp.int32)
    position = iota((capacity, columns), 1)
    for sender in range(devices):
        match = asked[0:capacity, sender : sender + 1] == position
        chosen[sender * capacity : (sender + 1) * capacity, :] = hot(match)
    out_ref[...] = contract(chosen[...], rows[...], ((1,), (1,))).astype(jnp.bfloat16)


def radiation_kernel(
    row_slots, arrived_ref, place_ref, span_ref, path_ref, cloud_ref, planck_ref,
    table_lw_ref, table_sw_ref, frac_ref, solar_ref, lw_ref, sw_ref, surface_ref,
    column_ref, beam_t, diffuse_t, long_t, sum_a, sum_b, ground_ref,
):
    levels, columns = path_ref.shape
    g_lw, g_sw = table_lw_ref.shape[0], table_sw_ref.shape[0]
    slots = arrived_ref.shape[0]
    part = 512
    place = place_ref[...]
    total = None
    for start in range(0, slots, part):
        here = hot(place == iota((part, columns), 0) + start)
        term = contract(arrived_ref[start : start + part, :], here, ((0,), (0,)))
        total = term if total is None else total + term
    column_ref[...] = total
    base = 6 * levels
    tile = WIDE
    table = jnp.concatenate([table_lw_ref[...], table_sw_ref[...]], axis=0)

    def scalar(offset, count, cols):
        values = column_ref[base + offset : base + offset + 1, cols]
        for piece in range(1, count):
            values = values + column_ref[base + offset + piece : base + offset + piece + 1, cols]
        return values

    def column_tile(step, carry):
        cols = pl.ds(pl.multiple_of(step * tile, tile), tile)
        surface = scalar(0, 3, cols)
        cosine = scalar(3, 3, cols)
        albedo = scalar(6, 3, cols)
        sunlit = scalar(9, 1, cols)
        slant = -LOG2E / cosine
        entry = iota((PRESS, tile), 0)

        def absorb_level(level, carry):
            def row(first):
                return column_ref[pl.ds(first + level, 1), cols]

            w0, w1, w2, w3 = (row(k * levels) for k in range(4))
            press = row(5 * levels).astype(jnp.int32)
            temp = row(4 * levels)
            offset = entry - press
            zero = jnp.zeros((), jnp.float32)
            near = jnp.where(offset == 0, w0, jnp.where(offset == 1, w1, zero))
            wrap = offset == 1 - PRESS
            far = jnp.where(
                offset == 0, w2, jnp.where(offset == 1, w3, jnp.where(wrap, w1, zero))
            )
            last = jnp.where(wrap[0:16], w3, zero).astype(jnp.bfloat16)
            near = near.astype(jnp.bfloat16)
            far = far.astype(jnp.bfloat16)
            temp = jnp.broadcast_to(temp.astype(jnp.bfloat16), (16, tile))
            hits = [temp == jnp.full((), k, jnp.bfloat16) for k in range(TEMPS)]
            blank = jnp.zeros((16, tile), jnp.bfloat16)
            blocks = []
            for k in range(TEMPS):
                for sub in range(0, PRESS, 16):
                    rest = blank
                    if k >= 2 and sub == 0:
                        rest = jnp.where(hits[k - 2], last, rest)
                    if k >= 1:
                        rest = jnp.where(hits[k - 1], far[sub : sub + 16], rest)
                    blocks.append(jnp.where(hits[k], near[sub : sub + 16], rest))
            mixing = jnp.concatenate(blocks, axis=0)
            absorb = jnp.dot(table, mixing, preferred_element_type=jnp.float32)
            path = path_ref[pl.ds(level, 1), cols]
            cloud = cloud_ref[pl.ds(level, 1), cols]
            long_t[level] = jnp.exp2(
                absorb[:g_lw] * (path * DIFFUSE) + cloud * DIFFUSE
            )
            beam_t[level] = jnp.exp2(absorb[g_lw:] * (path * slant) + cloud * slant)
            diffuse_t[level] = jnp.exp2(
                absorb[g_lw:] * (path * DIFFUSE) + cloud * DIFFUSE
            )
            return carry

        lax.fori_loop(0, levels, absorb_level, 0)

        sum_a[...] = jnp.zeros_like(sum_a)
        sum_b[...] = jnp.zeros_like(sum_b)

        def fold(values):
            return jnp.sum(values.reshape(-1, 8, values.shape[-1]), axis=0)

        chunk = 32
        weight_sum = jnp.sum(frac_ref[...])
        planck = planck_ref[:, cols]

        for start in range(0, g_lw, chunk):
            g = slice(start, start + chunk)
            frac = jnp.broadcast_to(frac_ref[g, :], (chunk, tile))

            def planck_row(level):
                return planck_ref[pl.ds(level, 1), cols]

            def down(level, state):
                passed = state * long_t[level, g, :]
                sum_a[level] += fold(passed * frac)
                following = jnp.minimum(level + 1, levels - 1)
                return passed + (planck_row(level) - planck_row(following))

            state = jnp.broadcast_to(-planck_row(0), (chunk, tile))
            lax.fori_loop(0, levels, down, state, unroll=4)

            def up(back, state):
                level = levels - 1 - back
                passed = state * long_t[level, g, :]
                sum_b[level] += fold(passed * frac)
                following = jnp.maximum(level - 1, 0)
                return passed + (planck_row(level) - planck_row(following))

            state = jnp.broadcast_to(surface - planck_row(levels - 1), (chunk, tile))
            lax.fori_loop(0, levels, up, state, unroll=4)

        own = planck * weight_sum
        below = jnp.sum(sum_a[...], axis=1) + own
        above = jnp.sum(sum_b[...], axis=1) + own
        ground = surface * weight_sum
        entering_down = jnp.concatenate([jnp.zeros((1, tile), jnp.float32), below[:-1]], axis=0)
        entering_up = jnp.concatenate([above[1:], ground], axis=0)
        lw_ref[:, cols] = (entering_down - below) + (entering_up - above)

        sum_a[...] = jnp.zeros_like(sum_a)
        sum_b[...] = jnp.zeros_like(sum_b)
        for start in range(0, g_sw, chunk):
            g = slice(start, start + chunk)

            def sun_down(level, state):
                state = state * beam_t[level, g, :]
                sum_a[level] += fold(state)
                return state

            state = jnp.broadcast_to(solar_ref[g, :], (chunk, tile))
            state = lax.fori_loop(0, levels, sun_down, state, unroll=4)

            def sun_up(back, state):
                level = levels - 1 - back
                state = state * diffuse_t[level, g, :]
                sum_b[level] += fold(state)
                return state

            lax.fori_loop(0, levels, sun_up, state, unroll=4)

        beam = jnp.sum(sum_a[...], axis=1) * cosine
        reflect = albedo * cosine
        diffuse = jnp.sum(sum_b[...], axis=1) * reflect
        top = jnp.sum(solar_ref[...]) * cosine
        arriving = jnp.concatenate([top, beam[:-1]], axis=0)
        rising = jnp.concatenate([diffuse[1:], albedo * beam[-1:]], axis=0)
        heat = (arriving - beam) + (rising - diffuse)
        sw_ref[:, cols] = jnp.where(sunlit > 0.5, heat, 0.0)
        ground_ref[:, cols] = jnp.where(sunlit > 0.5, (1.0 - albedo) * beam[-1:], 0.0)
        return carry

    lax.fori_loop(0, columns // tile, column_tile, 0)

    groups = surface_ref.shape[0]
    every = pl.ds(0, columns)
    slot_high = scalar(10, 1, every).astype(jnp.int32)
    slot_low = scalar(11, 1, every).astype(jnp.int32)
    dyn_row = span_ref[...] // row_slots[0]
    home = dyn_row * (row_slots[1] // LANES) + slot_high
    at_home = home == iota((groups, columns), 0)
    at_lane = hot(slot_low == iota((LANES, columns), 0))
    total = None
    for piece in pieces(ground_ref[...]):
        spread = jnp.where(at_home, piece.astype(jnp.float32), 0.0).astype(jnp.bfloat16)
        term = contract(spread, at_lane, ((1,), (1,)))
        total = term if total is None else total + term
    surface_ref[...] = total


def params():
    return pltpu.CompilerParams(vmem_limit_bytes=56 * 1024 * 1024)


def shape_of(shape, dtype):
    return jax.ShapeDtypeStruct(shape, dtype)


def whereabouts():
    stripes = lax.axis_size("col")
    devices = lax.axis_size("dyn") * stripes
    return lax.axis_index("dyn") * stripes + lax.axis_index("col"), stripes, devices


def peer(flat, stripes):
    return (flat // stripes, flat % stripes)


def greet():
    me, stripes, devices = whereabouts()
    barrier = pltpu.get_barrier_semaphore()

    def signal(step, carry):
        pl.semaphore_signal(
            barrier, inc=1, device_id=peer((me + step) % devices, stripes),
            device_id_type=pl.DeviceIdType.MESH,
        )
        return carry

    lax.fori_loop(1, devices, signal, 0)
    pl.semaphore_wait(barrier, devices - 1)


def swap_blocks(source, landing, send, receive, own):
    me, stripes, devices = whereabouts()

    def copy_of(step):
        target = (me + step) % devices
        return pltpu.make_async_remote_copy(
            src_ref=source.at[target], dst_ref=landing.at[me],
            send_sem=send.at[step], recv_sem=receive.at[step],
            device_id=peer(target, stripes), device_id_type=pl.DeviceIdType.MESH,
        )

    def start(step, carry):
        copy_of(step).start()
        return carry

    def finish(step, carry):
        copy_of(step).wait()
        return carry

    kept = pltpu.make_async_copy(source.at[me], landing.at[me], own)
    kept.start()
    lax.fori_loop(1, devices, start, 0)
    lax.fori_loop(1, devices, finish, 0)
    kept.wait()


def swap_kernel(source, landing, send, receive, own):
    greet()
    swap_blocks(source, landing, send, receive, own)


def swap(values, ident):
    devices = values.shape[0]
    return pl.pallas_call(
        swap_kernel,
        out_shape=shape_of(values.shape, values.dtype),
        in_specs=[VMEM],
        out_specs=VMEM,
        scratch_shapes=[
            pltpu.SemaphoreType.DMA((devices,)),
            pltpu.SemaphoreType.DMA((devices,)),
            pltpu.SemaphoreType.DMA,
        ],
        compiler_params=pltpu.CompilerParams(collective_id=ident, has_side_effects=True),
    )(values)


def collect_kernel(source, total, landing, send, receive, own):
    greet()
    swap_blocks(source, landing, send, receive, own)
    total[...] = jnp.sum(landing[...], axis=0)


def collect(values, ident):
    devices = values.shape[0]
    return pl.pallas_call(
        collect_kernel,
        out_shape=shape_of(values.shape[1:], values.dtype),
        in_specs=[VMEM],
        out_specs=VMEM,
        scratch_shapes=[
            pltpu.VMEM(values.shape, values.dtype),
            pltpu.SemaphoreType.DMA((devices,)),
            pltpu.SemaphoreType.DMA((devices,)),
            pltpu.SemaphoreType.DMA,
        ],
        compiler_params=pltpu.CompilerParams(collective_id=ident, has_side_effects=True),
    )(values)


def body(
    planck_source, absorber_path, cloud_depth, span_map, surface_source, interp_index,
    interp_weight, sunlit, sw_slot, cos_zenith, albedo, table_lw, table_sw, planck_frac,
    solar_weight,
):
    levels, columns = planck_source.shape
    stripes = lax.axis_size("col")
    devices = lax.axis_size("dyn") * stripes
    capacity = 2 * columns // devices
    slots = devices * capacity
    span = span_map[None, :]
    labels, place = pl.pallas_call(
        functools.partial(plan_kernel, devices, capacity),
        out_shape=(
            shape_of((devices, LANES), jnp.float32),
            shape_of((1, columns), jnp.int32),
        ),
        in_specs=[VMEM],
        out_specs=(VMEM, VMEM),
        compiler_params=params(),
    )(span)
    asked = swap(labels[:, None, :], 1)[:, 0, :]
    packed = pl.pallas_call(
        functools.partial(pack_kernel, devices, capacity),
        out_shape=shape_of((slots, WIDE), jnp.bfloat16),
        in_specs=[VMEM] * 8,
        out_specs=VMEM,
        scratch_shapes=[
            pltpu.VMEM((WIDE, columns), jnp.bfloat16),
            pltpu.VMEM((slots, columns), jnp.bfloat16),
        ],
        compiler_params=params(),
    )(
        asked, interp_index, interp_weight.reshape(4 * levels, columns), surface_source[None, :],
        cos_zenith[None, :], albedo[None, :], sunlit[None, :], sw_slot[None, :],
    )
    arrived = swap(packed.reshape(devices, capacity, WIDE), 2).reshape(slots, WIDE)
    g_lw, g_sw = table_lw.shape[0], table_sw.shape[0]
    sw_all = devices * (columns // 2)
    row_slots = (stripes * columns, stripes * (columns // 2))
    heating_lw, heating_sw, surface = pl.pallas_call(
        functools.partial(radiation_kernel, row_slots),
        out_shape=(
            shape_of((levels, columns), jnp.float32),
            shape_of((levels, columns), jnp.float32),
            shape_of((sw_all // LANES, LANES), jnp.float32),
        ),
        in_specs=[VMEM] * 10,
        out_specs=(VMEM,) * 3,
        scratch_shapes=[
            pltpu.VMEM((WIDE, columns), jnp.float32),
            pltpu.VMEM((levels, g_sw, WIDE), jnp.float32),
            pltpu.VMEM((levels, g_sw, WIDE), jnp.float32),
            pltpu.VMEM((levels, g_lw, WIDE), jnp.float32),
            pltpu.VMEM((levels, 8, WIDE), jnp.float32),
            pltpu.VMEM((levels, 8, WIDE), jnp.float32),
            pltpu.VMEM((1, columns), jnp.float32),
        ],
        compiler_params=params(),
    )(
        arrived, place, span, absorber_path, cloud_depth, planck_source, table_lw, table_sw,
        planck_frac[:, None], solar_weight[:, None],
    )
    sw_surface = collect(surface.reshape(devices, -1, LANES), 3)
    return heating_lw, heating_sw, sw_surface.reshape(columns // 2)


def solution(mesh):
    wide = P(None, AXES)
    flat = P(AXES)
    in_specs = (
        wide, wide, wide, flat, flat, wide, P(None, None, AXES), flat, flat, flat, flat,
        P(), P(), P(), P(),
    )
    out_specs = (wide, wide, flat)
    return jax.shard_map(body, mesh=mesh, in_specs=in_specs, out_specs=out_specs, check_vma=False)
```

time: 720 us -> 155 us (0.22); the launches traced: 711 us -> 154 us
  local copies, waits for them, and re-layouts: 254 us -> 4.15 us
  other arithmetic: 191 us -> 0 us
  matrix products: 149 us -> 0 us
  Pallas kernels: 0 us -> 149 us
  starting transfers between devices: 64.5 us -> 0 us
  waiting for transfers between devices: 42.5 us -> 0 us
  loops' own time: 8.49 us -> 0 us
    pallas_call x0 -> x6, Pallas kernels: none -> 149 us  [the longest x1 92.2 us: body(): pl.pallas_call(functools.partial(radiation_kernel, row_slots), out_shape=...]
    dot_general x96 -> x0, matrix products: 149 us -> none  [optical_depth(): jnp.dot(table, corner_weights(index_row, weight_rows), preferred_element_...]
    reduce_sum x99 -> x0, other arithmetic: 123 us -> none  [the longest x64 81.8 us: longwave_upward(): return (flux_out, jnp.sum(flux_in - flux_out, axis=0))]
    gather x28 -> x0, local copies, waits for them, and re-layouts: 107 us -> none  [the longest x16 80 us: gather_cols(): return jnp.take(values, index, axis=-1, mode='fill', fill_value=blank)]
    all_to_all x14 -> x0, starting transfers between devices: 64.5 us -> none  [the longest x1 7.28 us: body(): lax.all_to_all(gather_cols(cos_zenith[None, :], sw_filler, 1.0), 'col', s...]
    dynamic_update_slice x256 -> x0, local copies, waits for them, and re-layouts: 63 us -> none  [longwave(): lax.scan(longwave_downward, initial, (index_cols, weight_levels, path_col...]
    all_to_all x14 -> x0, waiting for transfers between devices: 42.5 us -> none  [the longest x1 9.3 us: body(): lax.all_to_all(sw_back, ('dyn', 'col'), split_axis=1, concat_axis=1, tile...]
    slice x98 -> x0, local copies, waits for them, and re-layouts: 31.3 us -> none  [the longest x96 31.1 us: corner_weights(): weight_rows[corner][None, :]]
  transfers between devices with their start and end apart: 14 -> 0, of which waited for: 8 -> 0; matrix products, arithmetic and copies ran while one was open for 53% -> 0% of each run, Pallas kernels for 0% -> 0%
where the time goes in v1:
time: 155 us; the launch traced here: 154 us
  Pallas kernels  149 us (96%)
  local copies, waits for them, and re-layouts  4.15 us (3%)
    pallas_call x1, Pallas kernels, body(): pl.pallas_call(functools.partial(radiation_kernel, row_slots), out_shape=...  92.2 us
    pallas_call x2, Pallas kernels, swap(): pl.pallas_call(swap_kernel, out_shape=shape_of(values.shape, values.dtype...  41.3 us
    pallas_call x1, Pallas kernels, collect(): pl.pallas_call(collect_kernel, out_shape=shape_of(values.shape[1:], value...  10.4 us
    pallas_call x1, Pallas kernels, body(): pl.pallas_call(functools.partial(pack_kernel, devices, capacity), out_sha...  3.5 us

profile of v1, /device:TPU:0, one launch (start us, length us, event | category | flops | bytes accessed | tf_op | source)
XLA Modules:
  0.0 154.1 jit_solution(3891210242337225530)
XLA Ops:
  0.6 1.9 %shard_map.166 = (f32[32,128]{1,0:T(8,128)}, s32[1,1024]{1,0:T(1,128)}) custom-call(s32[1,1024]{1,0:T(1,128)} %bitcast.20), custom_call_target="tpu_custom_call" | custom-call | tf_op jit(solution)/shard_map/pallas_call | solution.py:382
  2.5 11.4 %shard_map.167 = f32[32,1,128]{2,1,0:T(1,128)} custom-call(f32[32,1,128]{2,1,0:T(1,128)} %bitcast.22), custom_call_target="tpu_custom_call" | custom-call | tf_op jit(solution)/shard_map/pallas_call | solution.py:334
  13.9 3.5 %shard_map.168 = bf16[2048,256]{1,0:T(8,128)(2,1)} custom-call(f32[32,128]{1,0:T(8,128)} %bitcast.18, s32[32,1024]{1,0:T(8,128)} %index_ref.1, bf16[128,1024]{1,0:T(8,128)(2,1)} %bitcast.17, f32[1,1024]{1,0:T(1,128)} %bitcast.24, f32[1,1024]{1,0:T(1,128)} %bitcast.25, f32[1,1024]{1,0:T(1,128)} %bitcast.26, s32[1,1024]{1,0:T(1,128)} %bitcast.27, ...), custom_call_target="tpu_custom_call" | custom-call | tf_op jit(solution)/shard_map/pallas_call | solution.py:393
  17.4 29.9 %shard_map.169 = bf16[32,64,256]{2,1,0:T(8,128)(2,1)} custom-call(bf16[32,64,256]{2,1,0:T(8,128)(2,1)} %bitcast.16), custom_call_target="tpu_custom_call" | custom-call | tf_op jit(solution)/shard_map/pallas_call | solution.py:334
  47.3 0.0 copy-start.1
  47.4 0.7 copy-done.1
  48.0 0.8 copy.18.frac_ref
  48.8 0.0 copy-start.2
  48.8 0.7 copy-done.2
  49.5 0.8 copy.19.solar_ref
  50.3 92.2 %shard_map.170 = (f32[32,1024]{1,0:T(8,128)}, f32[32,1024]{1,0:T(8,128)}, f32[128,128]{1,0:T(8,128)}) custom-call(bf16[2048,256]{1,0:T(8,128)(2,1)} %bitcast.15, s32[1,1024]{1,0:T(1,128)} %get-tuple-element.9.place_ref, s32[1,1024]{1,0:T(1,128)} %bitcast.21, f32[32,1024]{1,0:T(8,128)} %path_ref.1, f32[32,1024]{1,0:T(8,128)} %cloud_ref.1, ...), custom_call_target="tpu_custom_call" | custom-call | tf_op jit(solution)/shard_map/pallas_call | solution.py:411
  142.4 10.4 %shard_map.171 = f32[4,128]{1,0:T(4,128)} custom-call(f32[32,4,128]{2,1,0:T(4,128)} %bitcast.19), custom_call_target="tpu_custom_call" | custom-call | tf_op jit(solution)/shard_map/pallas_call | solution.py:356
  152.9 0.0 copy-start
  152.9 0.7 copy-done
  153.6 0.6 copy.21
Async XLA Ops:
  47.3 0.7 copy-start.1
  48.8 0.7 copy-start.2
  152.9 0.7 copy-start

commit v2 on v1

v2 whole, which is shorter than its diff:
```python
import functools
import math

import jax
import jax.numpy as jnp
from jax import lax
from jax.experimental import pallas as pl
from jax.experimental.pallas import tpu as pltpu
from jax.sharding import PartitionSpec as P

TEMPS = 14
PRESS = 64
LANES = 128
WIDE = 256
HALF = 64
DARK = 128
AXES = ("dyn", "col")
LOG2E = math.log2(math.e)
DIFFUSE = -1.66 * LOG2E
VMEM = pl.BlockSpec(memory_space=pltpu.VMEM)


def iota(shape, dim):
    return lax.broadcasted_iota(jnp.int32, shape, dim)


def hot(mask):
    return jnp.where(mask, 1.0, 0.0).astype(jnp.bfloat16)


def contract(a, b, dims):
    return lax.dot_general(a, b, (dims, ((), ())), preferred_element_type=jnp.float32)


def pieces(values):
    high = values.astype(jnp.bfloat16)
    rest = values - high.astype(jnp.float32)
    middle = rest.astype(jnp.bfloat16)
    low = (rest - middle.astype(jnp.float32)).astype(jnp.bfloat16)
    return high, middle, low


def whereabouts():
    stripes = lax.axis_size("col")
    devices = lax.axis_size("dyn") * stripes
    return lax.axis_index("dyn") * stripes + lax.axis_index("col"), stripes, devices


def peer(flat, stripes):
    return (flat // stripes, flat % stripes)


def call_out():
    me, stripes, devices = whereabouts()
    barrier = pltpu.get_barrier_semaphore()

    def signal(step, carry):
        pl.semaphore_signal(
            barrier, inc=1, device_id=peer((me + step) % devices, stripes),
            device_id_type=pl.DeviceIdType.MESH,
        )
        return carry

    lax.fori_loop(1, devices, signal, 0)


def hear_all():
    devices = whereabouts()[2]
    pl.semaphore_wait(pltpu.get_barrier_semaphore(), devices - 1)


def swap_blocks(pairs, own):
    me, stripes, devices = whereabouts()

    def copy_of(step, source, landing, send, receive):
        target = (me + step) % devices
        return pltpu.make_async_remote_copy(
            src_ref=source.at[target], dst_ref=landing.at[me],
            send_sem=send.at[step], recv_sem=receive.at[step],
            device_id=peer(target, stripes), device_id_type=pl.DeviceIdType.MESH,
        )

    def start(step, carry):
        for pair in pairs:
            copy_of(step, *pair).start()
        return carry

    def finish(step, carry):
        for pair in pairs:
            copy_of(step, *pair).wait()
        return carry

    kept = [
        pltpu.make_async_copy(pair[0].at[me], pair[1].at[me], own.at[at])
        for at, pair in enumerate(pairs)
    ]
    for copy in kept:
        copy.start()
    lax.fori_loop(1, devices, start, 0)
    for copy in kept:
        copy.wait()
    lax.fori_loop(1, devices, finish, 0)


def fold_rows(capacity):
    return max(16, capacity // 2)


def plan(span, devices, capacity):
    columns = span.shape[1]
    target = span >> (columns.bit_length() - 1)
    where = span & (columns - 1)
    marked = target == iota((devices, columns), 0)
    before = hot(iota((columns, columns), 0) < iota((columns, columns), 1))
    counts = contract(hot(marked), before, ((1,), (0,)))
    rank = jnp.sum(jnp.where(marked, counts, 0.0), axis=0, keepdims=True).astype(jnp.int32)
    ranked = hot(rank == iota((LANES, columns), 0))
    high = jnp.where(marked, ((where >> 5) + 1).astype(jnp.float32), 0.0).astype(jnp.bfloat16)
    low = jnp.where(marked, (where & 31).astype(jnp.float32), 0.0).astype(jnp.bfloat16)
    dims = ((1,), (1,))
    labels = contract(high, ranked, dims) * 32.0 + contract(low, ranked, dims) - 32.0
    return labels, target * capacity + rank


def exchange_kernel(
    devices, capacity, span_ref, index_ref, weight_ref, surface_ref, cosine_ref, albedo_ref,
    sunlit_ref, slot_ref, heavy_ref, light_ref, place_ref,
    rows, chosen, heavy_out, light_out, label_out, label_in,
    label_send, label_receive, heavy_send, heavy_receive, light_send, light_receive, own,
):
    levels, columns = index_ref.shape
    call_out()
    labels, place = plan(span_ref[...], devices, capacity)
    place_ref[...] = place
    label_out[...] = labels[:, None, :]
    index = index_ref[...]
    rows[0 : 4 * levels, :] = weight_ref[...]
    cell = ((index & (PRESS - 1)) + PRESS) << (index >> 6)
    slot = slot_ref[...]
    scalars = [
        *pieces(surface_ref[...]),
        *pieces(cosine_ref[...]),
        *pieces(albedo_ref[...]),
        jnp.where(sunlit_ref[...] == 1, slot >> 7, DARK).astype(jnp.float32).astype(jnp.bfloat16),
        (slot & (LANES - 1)).astype(jnp.float32).astype(jnp.bfloat16),
    ]
    scalars = [values.astype(jnp.float32) for values in scalars]
    blank = jnp.zeros((HALF - levels - len(scalars), columns), jnp.float32)
    others = jnp.concatenate([cell.astype(jnp.float32)] + scalars + [blank], axis=0)
    others = others.astype(jnp.bfloat16)
    rows[4 * levels : 4 * levels + HALF, :] = others
    rows[4 * levels + HALF :, :] = others
    hear_all()
    swap_blocks([(label_out, label_in, label_send, label_receive)], own)
    labels = label_in[...].reshape(devices, LANES)
    if devices < LANES:
        labels = jnp.concatenate(
            [labels, jnp.zeros((LANES - devices, LANES), jnp.float32)], axis=0
        )
    asked = jnp.transpose(labels).astype(jnp.int32)
    position = iota((capacity, columns), 1)
    for sender in range(devices):
        match = asked[0:capacity, sender : sender + 1] == position
        chosen[sender * capacity : (sender + 1) * capacity, :] = hot(match)
    packed = contract(chosen[...], rows[...], ((1,), (1,)))
    heavy_out[...] = packed[:, :LANES].reshape(devices, capacity, LANES).astype(jnp.bfloat16)
    folded = fold_rows(capacity)
    light = packed[:, LANES:].reshape(devices, capacity, LANES)
    if folded < capacity:
        left = iota((devices, folded, LANES), 2) < HALF
        light = jnp.where(left, light[:, :folded], light[:, folded:])
    light_out[...] = light.astype(jnp.bfloat16)
    swap_blocks(
        [
            (heavy_out, heavy_ref, heavy_send, heavy_receive),
            (light_out, light_ref, light_send, light_receive),
        ],
        own,
    )


def collect_kernel(source, total, landing, send, receive, own):
    call_out()
    hear_all()
    swap_blocks([(source, landing, send, receive)], own)
    total[...] = jnp.sum(landing[...], axis=0)


def collect(values, ident):
    devices = values.shape[0]
    return pl.pallas_call(
        collect_kernel,
        out_shape=shape_of(values.shape[1:], values.dtype),
        in_specs=[VMEM],
        out_specs=VMEM,
        scratch_shapes=[
            pltpu.VMEM(values.shape, values.dtype),
            pltpu.SemaphoreType.DMA((devices,)),
            pltpu.SemaphoreType.DMA((devices,)),
            pltpu.SemaphoreType.DMA((1,)),
        ],
        compiler_params=pltpu.CompilerParams(collective_id=ident, has_side_effects=True),
    )(values)


def radiation_kernel(
    row_slots, capacity, heavy_ref, light_ref, place_ref, span_ref, path_ref, cloud_ref,
    planck_ref, table_lw_ref, table_sw_ref, frac_ref, solar_ref, lw_ref, sw_ref, surface_ref,
    column_ref, beam_t, diffuse_t, long_t, lw_down, lw_up, sw_down, sw_up, ground_ref,
    solar_row, frac_lanes, solar_lanes, step_down, step_up,
):
    levels, columns = path_ref.shape
    g_lw, g_sw = table_lw_ref.shape[0], table_sw_ref.shape[0]
    place = place_ref[...]

    def pick(source, index):
        part = min(512, source.shape[0])
        total = None
        for start in range(0, source.shape[0], part):
            here = hot(index == iota((part, columns), 0) + start)
            term = contract(source[start : start + part, :], here, ((0,), (0,)))
            total = term if total is None else total + term
        return total

    heavy_rows = 4 * levels
    base = heavy_rows + levels
    press_base = heavy_rows + HALF
    column_ref[0:heavy_rows, :] = pick(heavy_ref, place)
    folded = fold_rows(capacity)
    sender = place >> (capacity.bit_length() - 1)
    rank = place & (capacity - 1)
    others = pick(light_ref, sender * folded + (rank & (folded - 1)))
    column_ref[heavy_rows:press_base, :] = jnp.where(
        rank < folded, others[:HALF], others[HALF:]
    )
    cell = column_ref[heavy_rows:base, :]
    temp = jnp.zeros_like(cell)
    shrink = jnp.ones_like(cell)
    for k in range(1, TEMPS):
        above = cell >= float(PRESS << k)
        temp = jnp.where(above, float(k), temp)
        shrink = jnp.where(above, 0.5**k, shrink)
    column_ref[heavy_rows:base, :] = temp
    column_ref[press_base : press_base + levels, :] = cell * shrink - float(PRESS)
    tile = WIDE
    table = jnp.concatenate([table_lw_ref[...], table_sw_ref[...]], axis=0)
    solar_row[...] = jnp.zeros_like(solar_row)
    solar_row[:, 0:g_sw] = solar_ref[...]
    frac_lanes[...] = jnp.transpose(jnp.broadcast_to(frac_ref[...], (LANES, g_lw)))
    solar_lanes[...] = jnp.transpose(jnp.broadcast_to(solar_row[...], (LANES, WIDE)))
    weight_sum = jnp.sum(frac_ref[...])
    solar_sum = jnp.sum(solar_ref[...])

    def scalar(offset, count, cols):
        values = column_ref[base + offset : base + offset + 1, cols]
        for piece in range(1, count):
            values = values + column_ref[base + offset + piece : base + offset + piece + 1, cols]
        return values

    def column_tile(step, carry):
        cols = pl.ds(pl.multiple_of(step * tile, tile), tile)
        surface = scalar(0, 3, cols)
        cosine = scalar(3, 3, cols)
        albedo = scalar(6, 3, cols)
        lit = scalar(9, 1, cols) < DARK
        slant = -LOG2E / cosine
        entry = iota((PRESS, tile), 0)

        def absorb_level(level, carry):
            def row(first):
                return column_ref[pl.ds(first + level, 1), cols]

            w0, w1, w2, w3 = (row(k * levels) for k in range(4))
            press = row(press_base).astype(jnp.int32)
            temp = row(4 * levels)
            offset = entry - press
            zero = jnp.zeros((), jnp.float32)
            near = jnp.where(offset == 0, w0, jnp.where(offset == 1, w1, zero))
            wrap = offset == 1 - PRESS
            far = jnp.where(
                offset == 0, w2, jnp.where(offset == 1, w3, jnp.where(wrap, w1, zero))
            )
            last = jnp.where(wrap[0:16], w3, zero).astype(jnp.bfloat16)
            near = near.astype(jnp.bfloat16)
            far = far.astype(jnp.bfloat16)
            temp = jnp.broadcast_to(temp.astype(jnp.bfloat16), (16, tile))
            hits = [temp == jnp.full((), k, jnp.bfloat16) for k in range(TEMPS)]
            blank = jnp.zeros((16, tile), jnp.bfloat16)
            blocks = []
            for k in range(TEMPS):
                for sub in range(0, PRESS, 16):
                    rest = blank
                    if k >= 2 and sub == 0:
                        rest = jnp.where(hits[k - 2], last, rest)
                    if k >= 1:
                        rest = jnp.where(hits[k - 1], far[sub : sub + 16], rest)
                    blocks.append(jnp.where(hits[k], near[sub : sub + 16], rest))
            mixing = jnp.concatenate(blocks, axis=0)
            absorb = jnp.dot(table, mixing, preferred_element_type=jnp.float32)
            path = path_ref[pl.ds(level, 1), cols]
            cloud = cloud_ref[pl.ds(level, 1), cols]
            long_t[level] = jnp.exp2(
                absorb[:g_lw] * (path * DIFFUSE) + cloud * DIFFUSE
            )
            beam_t[level] = jnp.exp2(absorb[g_lw:] * (path * slant) + cloud * slant)
            diffuse_t[level] = jnp.exp2(
                absorb[g_lw:] * (path * DIFFUSE) + cloud * DIFFUSE
            )
            return carry

        lax.fori_loop(0, levels, absorb_level, 0, unroll=4)

        for sums in (lw_down, lw_up, sw_down, sw_up):
            sums[...] = jnp.zeros_like(sums)
        planck = planck_ref[:, cols]
        level_gap = jnp.zeros((1, tile), jnp.float32)
        steps = planck[:-1] - planck[1:]
        step_down[...] = jnp.concatenate([-planck[:1], steps, level_gap], axis=0)[:, None, :]
        step_up[...] = jnp.concatenate(
            [level_gap, -steps, surface - planck[-1:]], axis=0
        )[:, None, :]
        quarter_lw, quarter_sw = g_lw // 4, g_sw // 4

        def fold(values):
            return jnp.sum(values.reshape(-1, 8, values.shape[-1]), axis=0)

        def fluxes(work, carry):
            quarter = work // 2
            half = work % 2
            lanes = pl.ds(pl.multiple_of(half * LANES, LANES), LANES)
            long_g = pl.ds(pl.multiple_of(quarter * quarter_lw, 8), quarter_lw)
            sun_g = pl.ds(pl.multiple_of(quarter * quarter_sw, 8), quarter_sw)
            frac = frac_lanes[long_g, :]

            def down(level, state):
                flux, beam = state
                passed = flux * long_t[level, long_g, lanes]
                beam = beam * beam_t[level, sun_g, lanes]
                lw_down[level, :, lanes] += fold(passed * frac)
                sw_down[level, :, lanes] += fold(beam)
                return passed + step_down[level + 1, :, lanes], beam

            flux = jnp.broadcast_to(step_down[0, :, lanes], (quarter_lw, LANES))
            flux, beam = lax.fori_loop(0, levels, down, (flux, solar_lanes[sun_g, :]), unroll=4)

            def up(back, state):
                flux, beam = state
                level = levels - 1 - back
                passed = flux * long_t[level, long_g, lanes]
                beam = beam * diffuse_t[level, sun_g, lanes]
                lw_up[level, :, lanes] += fold(passed * frac)
                sw_up[level, :, lanes] += fold(beam)
                return passed + step_up[level, :, lanes], beam

            flux = jnp.broadcast_to(step_up[levels, :, lanes], (quarter_lw, LANES))
            lax.fori_loop(0, levels, up, (flux, beam), unroll=4)
            return carry

        lax.fori_loop(0, 8, fluxes, 0)

        own = planck * weight_sum
        below = jnp.sum(lw_down[...], axis=1) + own
        above = jnp.sum(lw_up[...], axis=1) + own
        ground = surface * weight_sum
        entering_down = jnp.concatenate([jnp.zeros((1, tile), jnp.float32), below[:-1]], axis=0)
        entering_up = jnp.concatenate([above[1:], ground], axis=0)
        lw_ref[:, cols] = (entering_down - below) + (entering_up - above)

        beam = jnp.sum(sw_down[...], axis=1) * cosine
        reflect = albedo * cosine
        diffuse = jnp.sum(sw_up[...], axis=1) * reflect
        top = solar_sum * cosine
        arriving = jnp.concatenate([top, beam[:-1]], axis=0)
        rising = jnp.concatenate([diffuse[1:], albedo * beam[-1:]], axis=0)
        heat = (arriving - beam) + (rising - diffuse)
        sw_ref[:, cols] = jnp.where(lit, heat, 0.0)
        ground_ref[:, cols] = jnp.where(lit, (1.0 - albedo) * beam[-1:], 0.0)
        return carry

    lax.fori_loop(0, columns // tile, column_tile, 0)

    groups = surface_ref.shape[0]
    every = pl.ds(0, columns)
    slot_high = scalar(9, 1, every).astype(jnp.int32)
    slot_low = scalar(10, 1, every).astype(jnp.int32)
    dyn_row = span_ref[...] // row_slots[0]
    home = dyn_row * (row_slots[1] // LANES) + slot_high
    at_home = home == iota((groups, columns), 0)
    at_lane = hot(slot_low == iota((LANES, columns), 0))
    total = None
    for piece in pieces(ground_ref[...]):
        spread = jnp.where(at_home, piece.astype(jnp.float32), 0.0).astype(jnp.bfloat16)
        term = contract(spread, at_lane, ((1,), (1,)))
        total = term if total is None else total + term
    surface_ref[...] = total


def params(**more):
    return pltpu.CompilerParams(vmem_limit_bytes=56 * 1024 * 1024, **more)


def shape_of(shape, dtype):
    return jax.ShapeDtypeStruct(shape, dtype)


def body(
    planck_source, absorber_path, cloud_depth, span_map, surface_source, interp_index,
    interp_weight, sunlit, sw_slot, cos_zenith, albedo, table_lw, table_sw, planck_frac,
    solar_weight,
):
    levels, columns = planck_source.shape
    stripes = lax.axis_size("col")
    devices = lax.axis_size("dyn") * stripes
    capacity = 2 * columns // devices
    slots = devices * capacity
    span = span_map[None, :]
    folded = fold_rows(capacity)
    link = pltpu.SemaphoreType.DMA((devices,))
    place_anywhere = pl.BlockSpec(memory_space=pl.ANY)
    heavy, light, place = pl.pallas_call(
        functools.partial(exchange_kernel, devices, capacity),
        out_shape=(
            shape_of((devices, capacity, LANES), jnp.bfloat16),
            shape_of((devices, folded, LANES), jnp.bfloat16),
            shape_of((1, columns), jnp.int32),
        ),
        in_specs=[VMEM] * 8,
        out_specs=(place_anywhere, place_anywhere, VMEM),
        scratch_shapes=[
            pltpu.VMEM((WIDE, columns), jnp.bfloat16),
            pltpu.VMEM((slots, columns), jnp.bfloat16),
            pltpu.VMEM((devices, capacity, LANES), jnp.bfloat16),
            pltpu.VMEM((devices, folded, LANES), jnp.bfloat16),
            pltpu.VMEM((devices, 1, LANES), jnp.float32),
            pltpu.VMEM((devices, 1, LANES), jnp.float32),
            *[link] * 6,
            pltpu.SemaphoreType.DMA((2,)),
        ],
        compiler_params=params(collective_id=1, has_side_effects=True),
    )(
        span, interp_index, interp_weight.reshape(4 * levels, columns), surface_source[None, :],
        cos_zenith[None, :], albedo[None, :], sunlit[None, :], sw_slot[None, :],
    )
    g_lw, g_sw = table_lw.shape[0], table_sw.shape[0]
    sw_all = devices * (columns // 2)
    row_slots = (stripes * columns, stripes * (columns // 2))
    heating_lw, heating_sw, surface = pl.pallas_call(
        functools.partial(radiation_kernel, row_slots, capacity),
        out_shape=(
            shape_of((levels, columns), jnp.float32),
            shape_of((levels, columns), jnp.float32),
            shape_of((sw_all // LANES, LANES), jnp.float32),
        ),
        in_specs=[VMEM] * 11,
        out_specs=(VMEM,) * 3,
        scratch_shapes=[
            pltpu.VMEM((WIDE, columns), jnp.float32),
            pltpu.VMEM((levels, g_sw, WIDE), jnp.float32),
            pltpu.VMEM((levels, g_sw, WIDE), jnp.float32),
            pltpu.VMEM((levels, g_lw, WIDE), jnp.float32),
            *[pltpu.VMEM((levels, 8, WIDE), jnp.float32)] * 4,
            pltpu.VMEM((1, columns), jnp.float32),
            pltpu.VMEM((1, WIDE), jnp.float32),
            pltpu.VMEM((g_lw, LANES), jnp.float32),
            pltpu.VMEM((WIDE, LANES), jnp.float32),
            *[pltpu.VMEM((levels + 1, 1, WIDE), jnp.float32)] * 2,
        ],
        compiler_params=params(),
    )(
        heavy.reshape(slots, LANES), light.reshape(devices * folded, LANES), place, span, absorber_path, cloud_depth, planck_source, table_lw, table_sw,
        planck_frac[None, :], solar_weight[None, :],
    )
    sw_surface = collect(surface.reshape(devices, -1, LANES), 2)
    return heating_lw, heating_sw, sw_surface.reshape(columns // 2)


def solution(mesh):
    wide = P(None, AXES)
    flat = P(AXES)
    in_specs = (
        wide, wide, wide, flat, flat, wide, P(None, None, AXES), flat, flat, flat, flat,
        P(), P(), P(), P(),
    )
    out_specs = (wide, wide, flat)
    return jax.shard_map(body, mesh=mesh, in_specs=in_specs, out_specs=out_specs, check_vma=False)
```

time: 155 us -> 114 us (0.74)
  Pallas kernels: 149 us -> 111 us
  local copies, waits for them, and re-layouts: 4.15 us -> 1.23 us
    pallas_call x5 -> x2, Pallas kernels: 139 us -> 102 us  [the longest x1 67.2 us: body(): pl.pallas_call(functools.partial(radiation_kernel, row_slots, capacity),...]
    broadcast_in_dim x2 -> x0, local copies, waits for them, and re-layouts: 1.56 us -> none  [the longest x1 0.79 us: body(): planck_frac[:, None]]
where the time goes in v2:
time: 114 us; the launch traced here: 113 us
  Pallas kernels  111 us (97%)
  local copies, waits for them, and re-layouts  1.23 us (1%)
    pallas_call x1, Pallas kernels, body(): pl.pallas_call(functools.partial(radiation_kernel, row_slots, capacity),...  67.2 us
    pallas_call x1, Pallas kernels, body(): pl.pallas_call(functools.partial(exchange_kernel, devices, capacity), out...  34.5 us
    pallas_call x1, Pallas kernels, collect(): pl.pallas_call(collect_kernel, out_shape=shape_of(values.shape[1:], value...  9.65 us

profile of v2, /device:TPU:0, one launch (start us, length us, event | category | flops | bytes accessed | tf_op | source)
XLA Modules:
  0.0 113.3 jit_solution(11091427300114438822)
XLA Ops:
  0.6 34.5 %shard_map.166 = (bf16[32,64,128]{2,1,0:T(8,128)(2,1)}, bf16[32,32,128]{2,1,0:T(8,128)(2,1)}, s32[1,1024]{1,0:T(1,128)}) custom-call(s32[1,1024]{1,0:T(1,128)} %bitcast.17, s32[32,1024]{1,0:T(8,128)} %index_ref.1, bf16[128,1024]{1,0:T(8,128)(2,1)} %bitcast.15, f32[1,1024]{1,0:T(1,128)} %bitcast.20, f32[1,1024]{1,0:T(1,128)} %bitcast.21, f32[1,1024]{1,0:T(1,128)} %bitcast.22, ...), custom_call_target="tpu_custom_call" | custom-call | tf_op jit(solution)/shard_map/pallas_call | solution.py:420
  35.2 67.2 %shard_map.167 = (f32[32,1024]{1,0:T(8,128)}, f32[32,1024]{1,0:T(8,128)}, f32[128,128]{1,0:T(8,128)}) custom-call(bf16[2048,128]{1,0:T(8,128)(2,1)} %bitcast.13, bf16[1024,128]{1,0:T(8,128)(2,1)} %bitcast.14, s32[1,1024]{1,0:T(1,128)} %get-tuple-element.11.place_ref, s32[1,1024]{1,0:T(1,128)} %bitcast.18, f32[32,1024]{1,0:T(8,128)} %path_ref.1, ...), custom_call_target="tpu_custom_call" | custom-call | tf_op jit(solution)/shard_map/pallas_call | solution.py:447
  102.4 9.6 %shard_map.168 = f32[4,128]{1,0:T(4,128)} custom-call(f32[32,4,128]{2,1,0:T(4,128)} %bitcast.16), custom_call_target="tpu_custom_call" | custom-call | tf_op jit(solution)/shard_map/pallas_call | solution.py:191
  112.0 1.2 %copy.19 = f32[512]{0:T(512)} copy(f32[512]{0:T(512)} %bitcast.19) | data formatting | bytes 4096

commit v3 on v2

--- a/solution.py
+++ b/solution.py
@@ -206,7 +206,7 @@
 def radiation_kernel(
     row_slots, capacity, heavy_ref, light_ref, place_ref, span_ref, path_ref, cloud_ref,
     planck_ref, table_lw_ref, table_sw_ref, frac_ref, solar_ref, lw_ref, sw_ref, surface_ref,
-    column_ref, beam_t, diffuse_t, long_t, lw_down, lw_up, sw_down, sw_up, ground_ref,
+    column_ref, flux_ref, beam_ref, diffuse_t, long_t, lw_down, lw_up, sw_down, sw_up, ground_ref,
     solar_row, frac_lanes, solar_lanes, step_down, step_up,
 ):
     levels, columns = path_ref.shape
@@ -266,7 +266,22 @@
         slant = -LOG2E / cosine
         entry = iota((PRESS, tile), 0)
 
+        planck = planck_ref[:, cols]
+        level_gap = jnp.zeros((1, tile), jnp.float32)
+        steps = planck[:-1] - planck[1:]
+        step_down[...] = jnp.concatenate([-planck[:1], steps, level_gap], axis=0)[:, None, :]
+        step_up[...] = jnp.concatenate(
+            [level_gap, -steps, surface - planck[-1:]], axis=0
+        )[:, None, :]
+        flux_ref[...] = jnp.broadcast_to(step_down[0], (g_lw, tile))
+        beam_ref[...] = jnp.concatenate([solar_lanes[0:g_sw, :]] * 2, axis=1)
+
+        def fold(values):
+            return jnp.sum(values.reshape(-1, 8, values.shape[-1]), axis=0)
+
         def absorb_level(level, carry):
+            frac = jnp.concatenate([frac_lanes[...]] * 2, axis=1)
+
             def row(first):
                 return column_ref[pl.ds(first + level, 1), cols]
 
@@ -299,10 +314,14 @@
             absorb = jnp.dot(table, mixing, preferred_element_type=jnp.float32)
             path = path_ref[pl.ds(level, 1), cols]
             cloud = cloud_ref[pl.ds(level, 1), cols]
-            long_t[level] = jnp.exp2(
-                absorb[:g_lw] * (path * DIFFUSE) + cloud * DIFFUSE
-            )
-            beam_t[level] = jnp.exp2(absorb[g_lw:] * (path * slant) + cloud * slant)
+            transmit = jnp.exp2(absorb[:g_lw] * (path * DIFFUSE) + cloud * DIFFUSE)
+            long_t[level] = transmit
+            passed = flux_ref[...] * transmit
+            lw_down[level] = fold(passed * frac)
+            flux_ref[...] = passed + step_down[level + 1]
+            beam = beam_ref[...] * jnp.exp2(absorb[g_lw:] * (path * slant) + cloud * slant)
+            sw_down[level] = fold(beam)
+            beam_ref[...] = beam
             diffuse_t[level] = jnp.exp2(
                 absorb[g_lw:] * (path * DIFFUSE) + cloud * DIFFUSE
             )
@@ -310,19 +329,9 @@
 
         lax.fori_loop(0, levels, absorb_level, 0, unroll=4)
 
-        for sums in (lw_down, lw_up, sw_down, sw_up):
+        for sums in (lw_up, sw_up):
             sums[...] = jnp.zeros_like(sums)
-        planck = planck_ref[:, cols]
-        level_gap = jnp.zeros((1, tile), jnp.float32)
-        steps = planck[:-1] - planck[1:]
-        step_down[...] = jnp.concatenate([-planck[:1], steps, level_gap], axis=0)[:, None, :]
-        step_up[...] = jnp.concatenate(
-            [level_gap, -steps, surface - planck[-1:]], axis=0
-        )[:, None, :]
         quarter_lw, quarter_sw = g_lw // 4, g_sw // 4
-
-        def fold(values):
-            return jnp.sum(values.reshape(-1, 8, values.shape[-1]), axis=0)
 
         def fluxes(work, carry):
             quarter = work // 2
@@ -331,17 +340,6 @@
             long_g = pl.ds(pl.multiple_of(quarter * quarter_lw, 8), quarter_lw)
             sun_g = pl.ds(pl.multiple_of(quarter * quarter_sw, 8), quarter_sw)
             frac = frac_lanes[long_g, :]
-
-            def down(level, state):
-                flux, beam = state
-                passed = flux * long_t[level, long_g, lanes]
-                beam = beam * beam_t[level, sun_g, lanes]
-                lw_down[level, :, lanes] += fold(passed * frac)
-                sw_down[level, :, lanes] += fold(beam)
-                return passed + step_down[level + 1, :, lanes], beam
-
-            flux = jnp.broadcast_to(step_down[0, :, lanes], (quarter_lw, LANES))
-            flux, beam = lax.fori_loop(0, levels, down, (flux, solar_lanes[sun_g, :]), unroll=4)
 
             def up(back, state):
                 flux, beam = state
@@ -353,7 +351,7 @@
                 return passed + step_up[level, :, lanes], beam
 
             flux = jnp.broadcast_to(step_up[levels, :, lanes], (quarter_lw, LANES))
-            lax.fori_loop(0, levels, up, (flux, beam), unroll=4)
+            lax.fori_loop(0, levels, up, (flux, beam_ref[sun_g, lanes]), unroll=4)
             return carry
 
         lax.fori_loop(0, 8, fluxes, 0)
@@ -455,7 +453,8 @@
         out_specs=(VMEM,) * 3,
         scratch_shapes=[
             pltpu.VMEM((WIDE, columns), jnp.float32),
-            pltpu.VMEM((levels, g_sw, WIDE), jnp.float32),
+            pltpu.VMEM((g_lw, WIDE), jnp.float32),
+            pltpu.VMEM((g_sw, WIDE), jnp.float32),
             pltpu.VMEM((levels, g_sw, WIDE), jnp.float32),
             pltpu.VMEM((levels, g_lw, WIDE), jnp.float32),
             *[pltpu.VMEM((levels, 8, WIDE), jnp.float32)] * 4,

time: 114 us -> 109 us (0.956)
  Pallas kernels: 111 us -> 107 us
    pallas_call x1, Pallas kernels: 67.2 us -> 63.2 us  [body(): pl.pallas_call(functools.partial(radiation_kernel, row_slots, capacity),...]
where the time goes in v3:
time: 109 us
  Pallas kernels  107 us (98%)
  local copies, waits for them, and re-layouts  1.23 us (1%)
    pallas_call x1, Pallas kernels, body(): pl.pallas_call(functools.partial(radiation_kernel, row_slots, capacity),...  63.2 us
    pallas_call x1, Pallas kernels, body(): pl.pallas_call(functools.partial(exchange_kernel, devices, capacity), out...  34.5 us
    pallas_call x1, Pallas kernels, collect(): pl.pallas_call(collect_kernel, out_shape=shape_of(values.shape[1:], value...  9.65 us

profile of v3, /device:TPU:0, one launch (start us, length us, event | category | flops | bytes accessed | tf_op | source)
XLA Modules:
  0.0 109.2 jit_solution(8145988612628386129)
XLA Ops:
  0.6 34.5 %shard_map.166 = (bf16[32,64,128]{2,1,0:T(8,128)(2,1)}, bf16[32,32,128]{2,1,0:T(8,128)(2,1)}, s32[1,1024]{1,0:T(1,128)}) custom-call(s32[1,1024]{1,0:T(1,128)} %bitcast.17, s32[32,1024]{1,0:T(8,128)} %index_ref.1, bf16[128,1024]{1,0:T(8,128)(2,1)} %bitcast.15, f32[1,1024]{1,0:T(1,128)} %bitcast.20, f32[1,1024]{1,0:T(1,128)} %bitcast.21, f32[1,1024]{1,0:T(1,128)} %bitcast.22, ...), custom_call_target="tpu_custom_call" | custom-call | tf_op jit(solution)/shard_map/pallas_call | solution.py:418
  35.2 63.2 %shard_map.167 = (f32[32,1024]{1,0:T(8,128)}, f32[32,1024]{1,0:T(8,128)}, f32[128,128]{1,0:T(8,128)}) custom-call(bf16[2048,128]{1,0:T(8,128)(2,1)} %bitcast.13, bf16[1024,128]{1,0:T(8,128)(2,1)} %bitcast.14, s32[1,1024]{1,0:T(1,128)} %get-tuple-element.11.place_ref, s32[1,1024]{1,0:T(1,128)} %bitcast.18, f32[32,1024]{1,0:T(8,128)} %path_ref.1, ...), custom_call_target="tpu_custom_call" | custom-call | tf_op jit(solution)/shard_map/pallas_call | solution.py:445
  98.3 9.6 %shard_map.168 = f32[4,128]{1,0:T(4,128)} custom-call(f32[32,4,128]{2,1,0:T(4,128)} %bitcast.16), custom_call_target="tpu_custom_call" | custom-call | tf_op jit(solution)/shard_map/pallas_call | solution.py:191
  108.0 1.2 %copy.19 = f32[512]{0:T(512)} copy(f32[512]{0:T(512)} %bitcast.19) | data formatting | bytes 4096

commit v4 on v3

--- a/solution.py
+++ b/solution.py
@@ -327,7 +327,7 @@
             )
             return carry
 
-        lax.fori_loop(0, levels, absorb_level, 0, unroll=4)
+        lax.fori_loop(0, levels, absorb_level, 0, unroll=8)
 
         for sums in (lw_up, sw_up):
             sums[...] = jnp.zeros_like(sums)
@@ -351,7 +351,7 @@
                 return passed + step_up[level, :, lanes], beam
 
             flux = jnp.broadcast_to(step_up[levels, :, lanes], (quarter_lw, LANES))
-            lax.fori_loop(0, levels, up, (flux, beam_ref[sun_g, lanes]), unroll=4)
+            lax.fori_loop(0, levels, up, (flux, beam_ref[sun_g, lanes]), unroll=8)
             return carry
 
         lax.fori_loop(0, 8, fluxes, 0)

time: 109 us -> 105 us (0.963)
  Pallas kernels: 107 us -> 102 us
    pallas_call x1, Pallas kernels: 63.2 us -> 58.3 us  [body(): pl.pallas_call(functools.partial(radiation_kernel, row_slots, capacity),...]
where the time goes in v4:
time: 105 us; the launch traced here: 104 us
  Pallas kernels  102 us (97%)
  local copies, waits for them, and re-layouts  1.23 us (1%)
    pallas_call x1, Pallas kernels, body(): pl.pallas_call(functools.partial(radiation_kernel, row_slots, capacity),...  58.3 us
    pallas_call x1, Pallas kernels, body(): pl.pallas_call(functools.partial(exchange_kernel, devices, capacity), out...  34.5 us
    pallas_call x1, Pallas kernels, collect(): pl.pallas_call(collect_kernel, out_shape=shape_of(values.shape[1:], value...  9.65 us

profile of v4, /device:TPU:0, one launch (start us, length us, event | category | flops | bytes accessed | tf_op | source)
XLA Modules:
  0.0 104.4 jit_solution(10356878931540914555)
XLA Ops:
  0.6 34.5 %shard_map.166 = (bf16[32,64,128]{2,1,0:T(8,128)(2,1)}, bf16[32,32,128]{2,1,0:T(8,128)(2,1)}, s32[1,1024]{1,0:T(1,128)}) custom-call(s32[1,1024]{1,0:T(1,128)} %bitcast.17, s32[32,1024]{1,0:T(8,128)} %index_ref.1, bf16[128,1024]{1,0:T(8,128)(2,1)} %bitcast.15, f32[1,1024]{1,0:T(1,128)} %bitcast.20, f32[1,1024]{1,0:T(1,128)} %bitcast.21, f32[1,1024]{1,0:T(1,128)} %bitcast.22, ...), custom_call_target="tpu_custom_call" | custom-call | tf_op jit(solution)/shard_map/pallas_call | solution.py:418
  35.2 58.3 %shard_map.167 = (f32[32,1024]{1,0:T(8,128)}, f32[32,1024]{1,0:T(8,128)}, f32[128,128]{1,0:T(8,128)}) custom-call(bf16[2048,128]{1,0:T(8,128)(2,1)} %bitcast.13, bf16[1024,128]{1,0:T(8,128)(2,1)} %bitcast.14, s32[1,1024]{1,0:T(1,128)} %get-tuple-element.11.place_ref, s32[1,1024]{1,0:T(1,128)} %bitcast.18, f32[32,1024]{1,0:T(8,128)} %path_ref.1, ...), custom_call_target="tpu_custom_call" | custom-call | tf_op jit(solution)/shard_map/pallas_call | solution.py:445
  93.5 9.6 %shard_map.168 = f32[4,128]{1,0:T(4,128)} custom-call(f32[32,4,128]{2,1,0:T(4,128)} %bitcast.16), custom_call_target="tpu_custom_call" | custom-call | tf_op jit(solution)/shard_map/pallas_call | solution.py:191
  103.1 1.2 %copy.19 = f32[512]{0:T(512)} copy(f32[512]{0:T(512)} %bitcast.19) | data formatting | bytes 4096
